TPU v7x, 32 devices: a whole 2x2x4 slice. The times are simulated.
32 devices in a mesh: wide: 8 (over y, x, core), narrow: 4 (over z).
Axes of the slice: x: 2, y: 2, z: 4, core: 2. Of those that a mesh axis runs over, the one named last changes fastest.
Arguments:
- constraint_rows: bfloat16 [512, 32, 1024], P(None, ('wide', 'narrow')), may hold values from -1 to 1
- metric: bfloat16 [1024, 1024], replicated, may hold values from -8 to 8, as said below
Outputs:
- factored: float32 [512, 32, 4, 256], P(None, 'wide', 'narrow')
Inputs may be any that keep to these rules, and one draw needn't show every extreme that they name: `metric`: symmetric and positive definite.
All inputs are finite; a program needn't handle non-finite values.
Results may differ from a plain program's by a relative error of at most 0.0052.
Values may be sent and summed in bfloat16 or wider, within the bound.
A program may use at most 64 MiB of HBM per device.

v0:
```python
import jax
import jax.numpy as jnp
from jax import lax
from jax.sharding import PartitionSpec as P

P_SIZE = 1024
PB = 256
NPANEL = 2


def left_solve(factor_low, right_side):
    return jax.scipy.linalg.solve_triangular(factor_low, right_side, lower=True)


def strip_major(schur_slab, strips):
    row_count = schur_slab.shape[0]
    strip_len = schur_slab.shape[1] // strips
    reordered = schur_slab.reshape(row_count, strip_len, strips).transpose(0, 2, 1)
    return reordered.reshape(row_count, 1, strips, strip_len)


def local(constraint_rows, metric):
    groups = lax.axis_size(("wide", "narrow"))
    strips = lax.axis_size("narrow")
    row_count = constraint_rows.shape[0]
    panel_depth = P_SIZE // groups
    block_rows = PB // groups
    flat_rows = constraint_rows[:, 0, :]
    projected = jnp.dot(flat_rows, metric, preferred_element_type=jnp.float32).astype(jnp.bfloat16)
    gram_cols = jnp.einsum(
        "rn,kmn->rkm",
        projected,
        lax.all_gather(constraint_rows[:panel_depth], ("wide", "narrow"), axis=1, tiled=True),
        preferred_element_type=jnp.float32,
    )
    schur_slab = (gram_cols * gram_cols).reshape(row_count, P_SIZE)
    grid_block = lax.all_to_all(
        strip_major(schur_slab, strips), "narrow", split_axis=2, concat_axis=1, tiled=True
    )
    strip_len = P_SIZE // strips
    grid_rows = row_count * strips
    narrow_panel = PB // strips
    own_strip = lax.axis_index("narrow")
    flat_block = grid_block.reshape(grid_rows, strip_len)
    for panel_number in range(NPANEL):
        col_begin = panel_number * PB
        row_begin = col_begin // groups
        strip_begin = col_begin // strips
        strip_end = strip_begin + narrow_panel
        own_rows = flat_block.reshape(row_count, strips, strip_len)[
            row_begin : row_begin + block_rows, :, strip_begin:
        ]
        shared = lax.all_gather(own_rows, "wide", axis=1, tiled=True)
        shared = shared.reshape(PB, strip_len - strip_begin)
        diag_strip, row_strip = (
            lax.all_gather(shared[:, :narrow_panel], "narrow", axis=1, tiled=True),
            lax.all_gather(flat_block[:, strip_begin:strip_end], "narrow", axis=1, tiled=True),
        )
        diag_block = diag_strip.reshape(PB, strips, narrow_panel).transpose(0, 2, 1).reshape(PB, PB)
        panel_cols = (
            row_strip.reshape(grid_rows, strips, narrow_panel)
            .transpose(0, 2, 1)
            .reshape(grid_rows, PB)
        )
        factor_low = jnp.linalg.cholesky(diag_block)
        upper_part = left_solve(factor_low, shared[:, narrow_panel:])
        column = left_solve(factor_low, panel_cols.T).T
        trailing = flat_block[:, strip_end:] - jnp.dot(
            column, upper_part, precision=lax.Precision.HIGHEST
        )
        own_cols = lax.dynamic_index_in_dim(
            column.reshape(grid_rows, narrow_panel, strips), own_strip, 2, keepdims=False
        )
        flat_block = jnp.concatenate([flat_block[:, :strip_begin], own_cols, trailing], axis=1)
    return flat_block.reshape(row_count, strips, 1, strip_len)


def solution(mesh):
    placed = (P(None, ("wide", "narrow"), None), P())
    return jax.shard_map(
        local,
        mesh=mesh,
        in_specs=placed,
        out_specs=P(None, "wide", "narrow", None),
        check_vma=False,
    )
```

profile of v0, /device:TPU:0, one launch (start us, length us, event | category | flops | bytes accessed | tf_op | source)
XLA Modules:
  0.0 370.1 jit_solution(5122359015492759876)
XLA Ops:
  6.5 1.6 slice.104
  8.2 61.3 %all-gather.5.cloned.1.call-done = bf16[32,32,1024]{2,0,1:T(8,128)(2,1)} async-done(((bf16[32,1,1024]{2,0,1:T(8,128)(2,1)}), bf16[32,32,1024]{2,0,1:T(8,128)(2,1)}) %all-gather.5.cloned.1.call-update) | async-done | bytes 2097168 | tf_op jit(solution)/shard_map/all_gather | solution.py:33
  69.5 5.7 %fusion.2 = f32[512,32,32]{0,2,1:T(8,128)} fusion(bf16[32,32,1024]{2,0,1:T(8,128)(2,1)} %all-gather.5.cloned.1.call-done, bf16[1024,1024]{1,0:T(8,128)(2,1)S(1)} %copy-done, bf16[512,1,1024]{2,0,1:T(8,128)(2,1)} %param.5), kind=kOutput, calls=%fused_computation.14 | convolution fusion | flops 2148532224 | bytes 7340032 | tf_op jit(solution)/shard_map/rn,kmn->rkm/dot_general | solution.py:30
  75.2 1.9 reshape_reshape.4
  77.1 1.8 copy.48
  78.9 52.5 %all_to_all.4 = f32[512,1,4,256]{3,0,1,2:T(8,128)S(1)} all-to-all(f32[512,1,4,256]{3,0,1,2:T(8,128)} %bitcast.137), channel_id=1, replica_groups=mesh['wide'=8,'narrow'=4] {'narrow'}, dimensions={2} | all-to-all | bytes 4194304 | tf_op jit(solution)/shard_map/all_to_all | solution.py:37
  131.4 1.3 copy-done.2
  132.7 2.7 copy.53
  135.4 2.0 reshape.92
  137.4 1.1 copy.54
  138.7 9.3 %all-gather = f32[8,1,32,256]{3,0,1,2:T(8,128)S(1)} all-gather(f32[8,1,4,256]{3,0,1,2:T(8,128)S(1)} %slice-done), channel_id=2, replica_groups=mesh['wide'=8,'narrow'=4] {'wide'}, dimensions={2}, use_global_device_ids=true | all-gather | bytes 294912 | tf_op jit(solution)/shard_map/all_gather | solution.py:53
  148.1 1.9 slice.153
  150.2 16.8 %all_gather.23 = f32[256,256]{0,1:T(8,128)S(1)} all-gather(f32[256,64]{0,1:T(8,128)S(1)} %copy.50), channel_id=1, replica_groups=mesh['wide'=8,'narrow'=4] {'narrow'}, dimensions={1}, use_global_device_ids=true | all-gather | bytes 327680 | tf_op jit(solution)/shard_map/all_gather | solution.py:56
  167.5 11.7 %cholesky.130 = f32[128,128]{1,0:T(8,128)S(1)} custom-call(f32[128,128]{1,0:T(8,128)S(1)} %cholesky.194), custom_call_target="Cholesky" | custom-call | tf_op jit(solution)/shard_map/jit(cholesky)/cholesky | solution.py:65
  179.2 9.8 %custom-call.23 = f32[1,128,128]{1,2,0:T(8,128)S(1)} custom-call(f32[1,128,128]{2,1,0:T(8,128)S(1)} %get-tuple-element.66), custom_call_target="InvertDiagBlocksLowerTriangular" | custom-call | tf_op jit(solution)/shard_map/jit(cholesky)/cholesky | solution.py:65
  189.6 11.7 %cholesky.147 = f32[128,128]{1,0:T(8,128)S(1)} custom-call(f32[128,128]{1,0:T(8,128)S(1)} %convolution_subtract_fusion.7), custom_call_target="Cholesky" | custom-call | tf_op jit(solution)/shard_map/jit(cholesky)/cholesky | solution.py:65
  203.3 4.1 %while.6 = (s32[]{:T(128)}, f32[256,256]{1,0:T(8,128)S(1)}, s32[2,2]{1,0:T(2,128)S(1)}, f32[2,128,128]{2,1,0:T(8,128)S(1)}, s32[]{:T(128)}) while((s32[]{:T(128)}, f32[256,256]{1,0:T(8,128)S(1)}, s32[2,2]{1,0:T(2,128)S(1)}, f32[2,128,128]{2,1,0:T(8,128)S(1)}, s32[]{:T(128)}) %tuple.49), condition=%wide.while_cond, body=%wide.while_body.sunk | while | flops 2 | bytes 131189 | solution.py:12
  204.2 1.3 bitcast_dynamic-update-slice_fusion.4
  206.1 1.3 bitcast_dynamic-update-slice_fusion.4
  207.5 19.7 %custom-call.24 = f32[2,128,128]{1,2,0:T(8,128)S(1)} custom-call(f32[2,128,128]{2,1,0:T(8,128)S(1)} %get-tuple-element.37), custom_call_target="InvertDiagBlocksLowerTriangular" | custom-call | tf_op jit(solution)/shard_map/jit(_solve_triangular)/triangular_solve | solution.py:12
  227.2 1.7 copy.71
  229.9 2.9 copy.55
  232.8 1.7 reshape.94
  234.5 2.4 fusion.10
  239.0 1.5 fusion.6
  241.0 1.7 convolution_subtract_fusion
  244.8 8.4 %all_gather.25 = f32[8,32,192]{2,0,1:T(8,128)S(1)} all-gather(f32[8,4,192]{2,0,1:T(8,128)S(1)} %copy.60), channel_id=1, replica_groups=mesh['wide'=8,'narrow'=4] {'wide'}, dimensions={1}, use_global_device_ids=true | all-gather | bytes 221184 | tf_op jit(solution)/shard_map/all_gather | solution.py:53
  254.1 15.1 %all_gather.26 = f32[256,256]{0,1:T(8,128)S(1)} all-gather(f32[256,64]{0,1:T(8,128)S(1)} %copy.62), channel_id=1, replica_groups=mesh['wide'=8,'narrow'=4] {'narrow'}, dimensions={1}, use_global_device_ids=true | all-gather | bytes 327680 | tf_op jit(solution)/shard_map/all_gather | solution.py:56
  269.2 1.8 reshape.95
  271.5 11.7 %cholesky.164 = f32[128,128]{1,0:T(8,128)S(1)} custom-call(f32[128,128]{1,0:T(8,128)S(1)} %cholesky.197), custom_call_target="Cholesky" | custom-call | tf_op jit(solution)/shard_map/jit(cholesky)/cholesky | solution.py:65
  283.3 9.8 %custom-call.25 = f32[1,128,128]{1,2,0:T(8,128)S(1)} custom-call(f32[1,128,128]{2,1,0:T(8,128)S(1)} %get-tuple-element.62), custom_call_target="InvertDiagBlocksLowerTriangular" | custom-call | tf_op jit(solution)/shard_map/jit(cholesky)/cholesky | solution.py:65
  293.6 11.7 %cholesky.181 = f32[128,128]{1,0:T(8,128)S(1)} custom-call(f32[128,128]{1,0:T(8,128)S(1)} %convolution_subtract_fusion.6), custom_call_target="Cholesky" | custom-call | tf_op jit(solution)/shard_map/jit(cholesky)/cholesky | solution.py:65
  308.0 4.0 %while.7 = (s32[]{:T(128)}, f32[256,256]{1,0:T(8,128)S(1)}, s32[2,2]{1,0:T(2,128)S(1)}, f32[2,128,128]{2,1,0:T(8,128)S(1)}, s32[]{:T(128)}) while((s32[]{:T(128)}, f32[256,256]{1,0:T(8,128)S(1)}, s32[2,2]{1,0:T(2,128)S(1)}, f32[2,128,128]{2,1,0:T(8,128)S(1)}, s32[]{:T(128)}) %tuple.61), condition=%wide.while_cond.clone, body=%wide.while_body.clone.sunk | while | flops 2 | bytes 131189 | solution.py:12
  308.7 1.3 bitcast_dynamic-update-slice_fusion.5
  310.7 1.3 bitcast_dynamic-update-slice_fusion.5
  312.0 20.1 %custom-call.26 = f32[2,128,128]{1,2,0:T(8,128)S(1)} custom-call(f32[2,128,128]{2,1,0:T(8,128)S(1)} %get-tuple-element.38), custom_call_target="InvertDiagBlocksLowerTriangular" | custom-call | tf_op jit(solution)/shard_map/jit(_solve_triangular)/triangular_solve | solution.py:12
  332.1 2.2 constant_dynamic-slice_fusion.3
  335.7 2.9 copy.78
  338.6 1.7 reshape.100
  340.4 2.4 fusion.8
  344.9 1.5 fusion.5
  346.9 2.3 convolution_subtract_fusion.1
  349.2 2.9 reshape.101
  352.1 2.1 constant_dynamic-slice_fusion.2
  354.3 1.3 copy.68
  355.6 1.4 copy.66
  357.0 2.8 pad_maximum_fusion.2
  359.9 3.5 copy.69
  (101 shorter events, 17.5 us)
Async XLA Ops:
  6.5 63.0 %copy-start = (bf16[1024,1024]{1,0:T(8,128)(2,1)S(1)}, bf16[1024,1024]{1,0:T(8,128)(2,1)}, u32[]{:S(2)}) copy-start(bf16[1024,1024]{1,0:T(8,128)(2,1)} %param.6) | copy-start | bytes 6291460
  6.5 63.0 %all-gather.5.cloned.1.call-start = ((), (), s32[]{:S(2)}) async-start(), calls=%async_computation.1 | async-start | bytes 2162688 | tf_op jit(solution)/shard_map/all_gather | solution.py:33
  8.2 221.7 %all-gather.7.cloned.1.call-start = ((), (), s32[]{:S(2)}) async-start(), calls=%async_computation.2 | async-start | bytes 2621440 | tf_op jit(solution)/shard_map/all_gather | solution.py:57
  131.4 1.3 copy-start.2
  137.4 1.3 slice-start
  138.6 197.1 %all-gather.9.cloned.1.call-start = ((), (), s32[]{:S(2)}) async-start(), calls=%async_computation.3 | async-start | bytes 2621440 | tf_op jit(solution)/shard_map/all_gather | solution.py:57
  167.3 59.9 %copy-start.3 = (f32[2048,192]{1,0:T(8,128)S(1)}, f32[2048,192]{1,0:T(8,128)}, u32[]{:S(2)}) copy-start(f32[2048,192]{1,0:T(8,128)} %slice.153) | copy-start | bytes 4718596
  234.5 2.4 copy-start.4
  239.0 2.0 copy-start.9
  242.7 1.2 copy-start.7
  242.7 26.5 %copy-start.6 = (f32[2048,256]{0,1:T(8,128)S(1)}, f32[2048,256]{0,1:T(8,128)}, u32[]{:S(2)}) copy-start(f32[2048,256]{0,1:T(8,128)} %fusion.6) | copy-start | bytes 6291460
  253.3 0.7 copy-start.11
  306.1 28.8 %copy-start.12 = (f32[8,32,192]{2,1,0:T(8,128)S(1)}, f32[8,32,192]{2,1,0:T(8,128)}, u32[]{:S(2)}) copy-start(f32[8,32,192]{2,1,0:T(8,128)} %copy-done.11) | copy-start | bytes 589828
  332.1 3.6 copy-start.13
  340.4 2.5 copy-start.5
  342.8 1.0 copy-start.14
  344.9 2.0 copy-start.8
  349.2 5.1 %copy-start.10 = (f32[2048,128]{0,1:T(8,128)S(1)}, f32[2048,128]{0,1:T(8,128)}, u32[]{:S(2)}) copy-start(f32[2048,128]{0,1:T(8,128)} %convolution_subtract_fusion.1) | copy-start | bytes 3145732
  357.0 6.3 %copy-start.1 = (bf16[1024,1024]{1,0:T(8,128)(2,1)S(1)}, bf16[1024,1024]{1,0:T(8,128)(2,1)}, u32[]{:S(2)}) copy-start(bf16[1024,1024]{1,0:T(8,128)(2,1)} %param.6) | copy-start | bytes 6291460
Sparse Core Ops, SparseCore 0:
  10.3 59.1 all-gather.4
  138.7 48.2 all-gather.6
  254.2 45.6 all-gather.8
where the time goes:
time: 376 us; the launch traced here: 370 us
  other arithmetic  114 us (30%)
  blocking collectives  102 us (27%)
  waiting for transfers between devices  61.4 us (16%)
  local copies, waits for them, and re-layouts  54.1 us (14%)
  matrix products  21.5 us (6%)
  between operations  16.4 us (4%)
    another operation x13, other arithmetic, local(): factor_low = jnp.linalg.cholesky(diag_block)  68.6 us
    all_gather x1, waiting for transfers between devices, local(): lax.all_gather(constraint_rows[:panel_depth], ('wide', 'narrow'), axis=1,...  61.3 us
    all_to_all x1, blocking collectives, local(): lax.all_to_all(strip_major(schur_slab, strips), 'narrow', split_axis=2, c...  52.5 us
    another operation x5, other arithmetic, left_solve(): return jax.scipy.linalg.solve_triangular(factor_low, right_side, lower=True)  39.8 us
    all_gather x2, blocking collectives, local(): lax.all_gather(shared[:, :narrow_panel], 'narrow', axis=1, tiled=True)  31.9 us
    all_gather x2, blocking collectives, local(): shared = lax.all_gather(own_rows, 'wide', axis=1, tiled=True)  17.6 us
    another operation x12, matrix products, left_solve(): return jax.scipy.linalg.solve_triangular(factor_low, right_side, lower=True)  10.7 us
    another operation x16, local copies, waits for them, and re-layouts, left_solve(): return jax.scipy.linalg.solve_triangular(factor_low, right_side, lower=True)  8.05 us
  transfers between devices with their start and end apart: 3, of which 1 were waited for; matrix products, arithmetic and copies ran while one was open for 35% of the time, Pallas kernels for 0%

commit v1 on v0

v1 whole, which is shorter than its diff:
```python
import functools

import jax
import jax.numpy as jnp
from jax import lax
from jax.experimental import pallas as pl
from jax.experimental.pallas import tpu as pltpu
from jax.sharding import PartitionSpec as P

P_SIZE = 1024
PB = 256
NPANEL = 2
DONE = PB * NPANEL
MESH = pl.DeviceIdType.MESH


def gather_kernel(n_wide, n_narrow, own_ref, out_ref, own_sem, send_sem, recv_sem):
    w, z = lax.axis_index("wide"), lax.axis_index("narrow")
    mates = [lax.rem(w + 2 * i, n_wide) for i in range(1, n_wide // 2)]
    twin = w + 1 - 2 * lax.rem(w, 2)
    column = [lax.rem(z + i, n_narrow) for i in range(1, n_narrow)]

    barrier = pltpu.get_barrier_semaphore()
    partners = [(w, p) for p in column] + [(m, z) for m in mates] + [(twin, z)]
    for partner in partners:
        pl.semaphore_signal(barrier, inc=1, device_id=partner, device_id_type=MESH)
    pl.semaphore_wait(barrier, len(partners))

    sent = []

    def send(src, slot, target):
        copy = pltpu.make_async_remote_copy(
            src_ref=src,
            dst_ref=out_ref.at[slot],
            send_sem=send_sem.at[len(sent)],
            recv_sem=recv_sem.at[slot],
            device_id=target,
            device_id_type=MESH,
        )
        copy.start()
        sent.append(copy)

    def arrived(slot):
        pltpu.make_async_remote_copy(
            src_ref=own_ref,
            dst_ref=out_ref.at[slot],
            send_sem=send_sem.at[0],
            recv_sem=recv_sem.at[slot],
            device_id=(twin, z),
            device_id_type=MESH,
        ).wait_recv()

    me = w * n_narrow + z
    for p in column:
        send(own_ref, me, (w, p))
    for m in mates:
        send(own_ref, me, (m, z))
    send(own_ref, me, (twin, z))
    keep = pltpu.make_async_copy(own_ref, out_ref.at[me], own_sem)
    keep.start()
    for p in column:
        slot = w * n_narrow + p
        arrived(slot)
        for m in mates:
            send(out_ref.at[slot], slot, (m, z))
        send(out_ref.at[slot], slot, (twin, z))
    for p in [z] + column:
        for m in mates:
            slot = m * n_narrow + p
            arrived(slot)
            send(out_ref.at[slot], slot, (twin, z))
    for p in [z] + column:
        for m in [w] + mates:
            arrived((m + 1 - 2 * lax.rem(m, 2)) * n_narrow + p)
    keep.wait()
    for copy in sent:
        copy.wait_send()


def gather_panel(own, n_wide, n_narrow):
    groups = n_wide * n_narrow
    return pl.pallas_call(
        functools.partial(gather_kernel, n_wide, n_narrow),
        out_shape=jax.ShapeDtypeStruct((groups,) + own.shape, own.dtype),
        in_specs=[pl.BlockSpec(memory_space=pltpu.VMEM)],
        out_specs=pl.BlockSpec(memory_space=pltpu.VMEM),
        scratch_shapes=[
            pltpu.SemaphoreType.DMA,
            pltpu.SemaphoreType.DMA((groups,)),
            pltpu.SemaphoreType.DMA((groups,)),
        ],
        compiler_params=pltpu.CompilerParams(
            collective_id=0, has_side_effects=True, vmem_limit_bytes=16 * 2**20
        ),
    )(own)


def product(a, b, dims=((1,), (0,))):
    return lax.dot_general(
        a, b, (dims, ((), ())), precision=lax.Precision.HIGHEST, preferred_element_type=jnp.float32
    )


def product_t(a, b):
    return product(a, b, ((1,), (1,)))


def spread_lane(x, lane):
    return jnp.broadcast_to(x[:, lane : lane + 1], x.shape)


def spread_row(x, row):
    return jnp.broadcast_to(x[row : row + 1, :], x.shape)


def inverse_low_base(block):
    size = block.shape[0]
    tiles = [block[8 * g : 8 * g + 8, :] for g in range(size // 8)]
    lane = lax.broadcasted_iota(jnp.int32, (8, size), 1)
    sub = lax.broadcasted_iota(jnp.int32, (8, size), 0)
    for g in range(size // 8):
        base = 8 * g
        inside = (lane >= base) & (lane < base + 8)
        later = range(g + 1, size // 8)
        cols = {h: [spread_lane(tiles[h], base + t) for t in range(8)] for h in [g, *later]}
        rows = jnp.where(inside, jnp.where(lane == base + sub, 1.0, 0.0), tiles[g])
        for h in later:
            tiles[h] = jnp.where(inside, 0.0, tiles[h])
        scale = jnp.zeros((8, size), jnp.float32)
        for t in range(8):
            pivots = [spread_row(cols[g][k], t) for k in range(t, 8)]
            row = spread_row(rows, t)
            inv = 1.0 / pivots[0]
            scale = jnp.where(sub == t, lax.rsqrt(pivots[0]), scale)
            factor = jnp.where(sub > t, cols[g][t] * inv, 0.0)
            rows = rows - factor * row
            for k in range(t + 1, 8):
                cols[g][k] = cols[g][k] - factor * pivots[k - t]
            for h in later:
                factor = cols[h][t] * inv
                tiles[h] = tiles[h] - factor * row
                for k in range(t + 1, 8):
                    cols[h][k] = cols[h][k] - factor * pivots[k - t]
        tiles[g] = jnp.where(lane < base + 8, rows, 0.0) * scale
    return jnp.concatenate(tiles, axis=0)


def inverse_low(block):
    size = block.shape[0]
    if size <= 128:
        return inverse_low_base(block)
    half = size // 2
    first = inverse_low(block[:half, :half])
    below = product_t(block[half:, :half], first)
    second = inverse_low(block[half:, half:] - product_t(below, below))
    corner = -product(second, product(below, first))
    top = jnp.concatenate([first, jnp.zeros_like(first)], axis=1)
    return jnp.concatenate([top, jnp.concatenate([corner, second], axis=1)], axis=0)


def symmetric(block):
    return 0.5 * (block + block.T)


def factor_kernel(strips, slab_ref, out_ref, solve_rows, solve_cols):
    strip = DONE // strips
    low0 = inverse_low(symmetric(slab_ref[:PB, :PB]))
    upper = product(low0, slab_ref[:PB, PB:DONE])
    column = product_t(slab_ref[PB:DONE, :PB], low0)
    low1 = inverse_low(symmetric(slab_ref[PB:DONE, PB:DONE] - product(column, upper)))
    zero = jnp.zeros((PB, PB), jnp.float32)
    by_strip = []
    for ref, cross in ((solve_rows, upper.T), (solve_cols, column)):
        below = jnp.concatenate([-product(low1, product(cross, low0)), low1], axis=1)
        solve = jnp.concatenate([jnp.concatenate([low0, zero], axis=1), below], axis=0)
        for c in range(DONE // 128):
            ref[c] = solve[:, c * 128 : (c + 1) * 128]
        chunks = []
        for c in range(DONE // 128):
            picked = [ref[c, pl.ds(s, strip, stride=strips), :] for s in range(strips)]
            chunks.append(jnp.concatenate(picked, axis=0))
        by_strip.append(jnp.concatenate(chunks, axis=1))
    upper_all = product(by_strip[1], slab_ref[:DONE, DONE:])
    columns = product_t(slab_ref[DONE:, :DONE], by_strip[0])
    trailing = slab_ref[DONE:, DONE:] - product(columns, upper_all)
    for s in range(strips):
        cut = slice(s * strip, (s + 1) * strip)
        out_ref[s, :, :strip] = columns[:, cut].astype(out_ref.dtype)
        out_ref[s, :, strip:] = trailing[:, cut].astype(out_ref.dtype)


def factor(slab, strips):
    row_count = slab.shape[0] - DONE
    return pl.pallas_call(
        functools.partial(factor_kernel, strips),
        out_shape=jax.ShapeDtypeStruct((strips, row_count, P_SIZE // strips), jnp.bfloat16),
        in_specs=[pl.BlockSpec(memory_space=pltpu.VMEM)],
        out_specs=pl.BlockSpec(memory_space=pltpu.VMEM),
        scratch_shapes=[pltpu.VMEM((DONE // 128, DONE, 128), jnp.float32)] * 2,
        compiler_params=pltpu.CompilerParams(vmem_limit_bytes=48 * 2**20),
    )(slab)


def local(constraint_rows, metric):
    n_wide, strips = lax.axis_size("wide"), lax.axis_size("narrow")
    groups = n_wide * strips
    depth = P_SIZE // groups
    order = metric.shape[0]
    own_rows = constraint_rows[:, 0, :]
    gathered = gather_panel(own_rows[:depth], n_wide, strips)
    gathered = gathered.reshape(n_wide, strips, depth, order)
    ahead = DONE // groups
    first = gathered[:, :, :ahead].transpose(2, 0, 1, 3).reshape(DONE, order)
    rest = gathered[:, :, ahead:].transpose(1, 2, 0, 3).reshape(P_SIZE - DONE, order)
    panel = jnp.concatenate([first, rest], axis=0)
    rows = jnp.concatenate([first, own_rows], axis=0)
    projected = jnp.dot(rows, metric, preferred_element_type=jnp.float32).astype(jnp.bfloat16)
    gram = lax.dot_general(
        projected, panel, (((1,), (1,)), ((), ())), preferred_element_type=jnp.float32
    )
    strips_out = factor(gram * gram, strips)
    mine = lax.all_to_all(strips_out, "narrow", split_axis=0, concat_axis=0, tiled=True)
    return mine.astype(jnp.float32).transpose(1, 0, 2)[:, :, None, :]


def solution(mesh):
    placed = (P(None, ("wide", "narrow"), None), P())
    return jax.shard_map(
        local,
        mesh=mesh,
        in_specs=placed,
        out_specs=P(None, "wide", "narrow", None),
        check_vma=False,
    )
```

time: 376 us -> 97.1 us (0.26); the launches traced: 370 us -> 96.9 us
  other arithmetic: 114 us -> 0.18 us
  blocking collectives: 102 us -> 29.8 us
  waiting for transfers between devices: 61.4 us -> 0 us
  Pallas kernels: 0 us -> 47.8 us
  local copies, waits for them, and re-layouts: 54.1 us -> 10.4 us
  between operations: 16.4 us -> 0.04 us
  matrix products: 21.5 us -> 8.6 us
    another operation x18 -> x0, other arithmetic: 108 us -> none  [the longest x13 68.6 us: local(): factor_low = jnp.linalg.cholesky(diag_block)]
    all_gather x3 -> x0, waiting for transfers between devices: 61.3 us -> none  [the longest x1 61.3 us: local(): lax.all_gather(constraint_rows[:panel_depth], ('wide', 'narrow'), axis=1,...]
    all_gather x4 -> x0, blocking collectives: 49.5 us -> none  [the longest x2 31.9 us: local(): lax.all_gather(shared[:, :narrow_panel], 'narrow', axis=1, tiled=True)]
    pallas_call x0 -> x2, Pallas kernels: none -> 47.8 us  [the longest x1 25.6 us: factor(): pl.pallas_call(functools.partial(factor_kernel, strips), out_shape=jax.Sh...]
    all_to_all x1, blocking collectives: 52.5 us -> 29.8 us  [local(): lax.all_to_all(strips_out, 'narrow', split_axis=0, concat_axis=0, tiled=T...]
    reshape x10 -> x1, local copies, waits for them, and re-layouts: 13.6 us -> 1.11 us  [local(): first = gathered[:, :, :ahead].transpose(2, 0, 1, 3).reshape(DONE, order)]
    another operation x22 -> x0, local copies, waits for them, and re-layouts: 11.8 us -> none  [the longest x16 8.05 us: left_solve(): return jax.scipy.linalg.solve_triangular(factor_low, right_side, lower=True)]
    another operation x16 -> x0, matrix products: 11.7 us -> none  [the longest x12 10.7 us: left_solve(): return jax.scipy.linalg.solve_triangular(factor_low, right_side, lower=True)]
  transfers between devices with their start and end apart: 3 -> 0, of which waited for: 1 -> 0; matrix products, arithmetic and copies ran while one was open for 35% -> 0% of each run, Pallas kernels for 0% -> 0%
where the time goes in v1:
time: 97.1 us; the launch traced here: 96.9 us
  Pallas kernels  47.8 us (49%)
  blocking collectives  29.8 us (31%)
  local copies, waits for them, and re-layouts  10.4 us (11%)
  matrix products  8.6 us (9%)
    all_to_all x1, blocking collectives, local(): lax.all_to_all(strips_out, 'narrow', split_axis=0, concat_axis=0, tiled=T...  29.8 us
    pallas_call x1, Pallas kernels, factor(): pl.pallas_call(functools.partial(factor_kernel, strips), out_shape=jax.Sh...  25.6 us
    pallas_call x1, Pallas kernels, gather_panel(): pl.pallas_call(functools.partial(gather_kernel, n_wide, n_narrow), out_sh...  22.2 us
    dot_general x1, matrix products, local(): lax.dot_general(projected, panel, (((1,), (1,)), ((), ())), preferred_ele...  8.6 us
    broadcast_in_dim x1, local copies, waits for them, and re-layouts, local(): return mine.astype(jnp.float32).transpose(1, 0, 2)[:, :, None, :]  3.48 us
    unnamed x4, local copies, waits for them, and re-layouts  2.19 us

profile of v1, /device:TPU:0, one launch (start us, length us, event | category | flops | bytes accessed | tf_op | source)
XLA Modules:
  0.0 96.9 jit_solution(4013892819727473873)
XLA Ops:
  0.0 0.0 copy-start
  0.0 1.0 %slice_bitcast_fusion.2.own_ref = bf16[32,1024]{1,0:T(8,128)(2,1)S(1)} fusion(bf16[512,1,1024]{2,0,1:T(8,128)(2,1)} %param.2), kind=kLoop, calls=%fused_computation.10 | loop fusion | bytes 131072 | tf_op jit(solution)/shard_map/slice | solution.py:210
  1.0 22.2 %shard_map.28 = bf16[32,32,1024]{2,1,0:T(8,128)(2,1)S(1)} custom-call(bf16[32,1024]{1,0:T(8,128)(2,1)S(1)} %slice_bitcast_fusion.2.own_ref), custom_call_target="tpu_custom_call" | custom-call | tf_op jit(solution)/shard_map/pallas_call | solution.py:82
  23.2 0.3 slice_bitcast_fusion
  23.5 1.6 %copy.4 = bf16[4,16,8,1024]{3,2,1,0:T(8,128)(2,1)} copy(bf16[4,16,8,1024]{3,1,0,2:T(8,128)(2,1)S(1)} %get-tuple-element.5) | data formatting | bytes 2097152 | tf_op jit(solution)/shard_map/transpose | solution.py:214
  25.1 0.8 copy.3
  25.9 1.1 %reshape.11 = bf16[512,1024]{1,0:T(8,128)(2,1)} reshape(bf16[16,8,4,1024]{3,2,1,0:T(4,128)(2,1)S(1)} %copy.3) | data formatting | bytes 2097152 | tf_op jit(solution)/shard_map/reshape | solution.py:213
  27.0 0.0 copy-done
  27.0 8.6 %convolution_multiply_fusion.slab_ref = f32[1024,1024]{1,0:T(8,128)} fusion(bf16[512,1024]{1,0:T(8,128)(2,1)} %reshape.11, bf16[512,1024]{1,0:T(8,128)(2,1)} %bitcast.15, bf16[1024,1024]{1,0:T(8,128)(2,1)S(1)} %copy-done, bf16[512,1024]{1,0:T(8,128)(2,1)} %bitcast.16), kind=kOutput, calls=%fused_computation | convolution fusion | flops 4305453056 | bytes 9437184 | tf_op jit(solution)/shard_map/dot_general | solution.py:218
  35.6 0.0 copy-start.1
  35.6 2.2 %copy-done.1 = f32[1024,1024]{1,0:T(8,128)S(1)} copy-done((f32[1024,1024]{1,0:T(8,128)S(1)}, f32[1024,1024]{1,0:T(8,128)}, u32[]{:S(2)}) %copy-start.1) | copy-done | bytes 4194328
  37.8 25.6 %shard_map.29 = bf16[4,512,256]{2,1,0:T(8,128)(2,1)S(1)} custom-call(f32[1024,1024]{1,0:T(8,128)S(1)} %copy-done.1), custom_call_target="tpu_custom_call" | custom-call | tf_op jit(solution)/shard_map/pallas_call | solution.py:194
  63.4 29.8 %all_to_all.5 = bf16[4,512,256]{2,1,0:T(8,128)(2,1)S(1)} all-to-all(bf16[4,512,256]{2,1,0:T(8,128)(2,1)S(1)} %shard_map.29), channel_id=1, replica_groups=mesh['wide'=8,'narrow'=4] {'narrow'}, dimensions={0} | all-to-all | bytes 2097152 | tf_op jit(solution)/shard_map/all_to_all | solution.py:222
  93.2 0.2 convert_bitcast_fusion
  93.4 3.5 %copy.5 = f32[512,4,1,256]{3,2,1,0:T(1,128)} copy(f32[512,4,1,256]{3,0,1,2:T(8,128)S(1)} %convert_bitcast_fusion) | data formatting | bytes 4194304 | tf_op jit(solution)/shard_map/broadcast_in_dim | solution.py:223
Async XLA Ops:
  0.0 27.0 %copy-start = (bf16[1024,1024]{1,0:T(8,128)(2,1)S(1)}, bf16[1024,1024]{1,0:T(8,128)(2,1)}, u32[]{:S(2)}) copy-start(bf16[1024,1024]{1,0:T(8,128)(2,1)} %param.3) | copy-start | bytes 6291460
  35.6 2.2 %copy-start.1 = (f32[1024,1024]{1,0:T(8,128)S(1)}, f32[1024,1024]{1,0:T(8,128)}, u32[]{:S(2)}) copy-start(f32[1024,1024]{1,0:T(8,128)} %convolution_multiply_fusion.slab_ref) | copy-start | bytes 12582916

commit v2 on v1

v2 whole, which is shorter than its diff:
```python
import functools

import jax
import jax.numpy as jnp
from jax import lax
from jax.experimental import pallas as pl
from jax.experimental.pallas import tpu as pltpu
from jax.sharding import PartitionSpec as P

P_SIZE = 1024
PB = 256
NPANEL = 2
DONE = PB * NPANEL
MESH = pl.DeviceIdType.MESH


def gather_kernel(n_wide, n_narrow, first_ref, rest_ref, firsts_ref, rests_ref, own_sem, send_sem, recv_sem):
    w, z = lax.axis_index("wide"), lax.axis_index("narrow")
    groups = n_wide * n_narrow
    mates = [lax.rem(w + 2 * i, n_wide) for i in range(1, n_wide // 2)]
    twin = w + 1 - 2 * lax.rem(w, 2)
    column = [lax.rem(z + i, n_narrow) for i in range(1, n_narrow)]

    barrier = pltpu.get_barrier_semaphore()
    partners = [(w, p) for p in column] + [(m, z) for m in mates] + [(twin, z)]
    for partner in partners:
        pl.semaphore_signal(barrier, inc=1, device_id=partner, device_id_type=MESH)
    pl.semaphore_wait(barrier, len(partners))

    sent = []

    def send(src, dst, sem, target):
        copy = pltpu.make_async_remote_copy(
            src_ref=src,
            dst_ref=dst,
            send_sem=send_sem.at[len(sent)],
            recv_sem=recv_sem.at[sem],
            device_id=target,
            device_id_type=MESH,
        )
        copy.start()
        sent.append(copy)

    def arrived(ref, sem):
        pltpu.make_async_remote_copy(
            src_ref=first_ref,
            dst_ref=ref,
            send_sem=send_sem.at[0],
            recv_sem=recv_sem.at[sem],
            device_id=(twin, z),
            device_id_type=MESH,
        ).wait_recv()

    me = w * n_narrow + z
    for p in column:
        send(first_ref, firsts_ref.at[me], me, (w, p))
    for m in mates:
        send(first_ref, firsts_ref.at[me], me, (m, z))
    send(first_ref, firsts_ref.at[me], me, (twin, z))
    keep = [
        pltpu.make_async_copy(first_ref, firsts_ref.at[me], own_sem.at[0]),
        pltpu.make_async_copy(rest_ref, rests_ref.at[w], own_sem.at[1]),
    ]
    for copy in keep:
        copy.start()
    for p in column:
        slot = w * n_narrow + p
        arrived(firsts_ref.at[slot], slot)
        for m in mates:
            send(firsts_ref.at[slot], firsts_ref.at[slot], slot, (m, z))
        send(firsts_ref.at[slot], firsts_ref.at[slot], slot, (twin, z))
    for m in mates + [twin]:
        send(rest_ref, rests_ref.at[w], groups + w, (m, z))
    for p in [z] + column:
        for m in mates:
            slot = m * n_narrow + p
            arrived(firsts_ref.at[slot], slot)
            send(firsts_ref.at[slot], firsts_ref.at[slot], slot, (twin, z))
    for m in mates:
        arrived(rests_ref.at[m], groups + m)
        send(rests_ref.at[m], rests_ref.at[m], groups + m, (twin, z))
    for m in [w] + mates:
        other = m + 1 - 2 * lax.rem(m, 2)
        for p in [z] + column:
            slot = other * n_narrow + p
            arrived(firsts_ref.at[slot], slot)
        arrived(rests_ref.at[other], groups + other)
    for copy in keep:
        copy.wait()
    for copy in sent:
        copy.wait_send()


def gather_panel(first, rest, n_wide, n_narrow):
    groups = n_wide * n_narrow
    in_vmem = pl.BlockSpec(memory_space=pltpu.VMEM)
    return pl.pallas_call(
        functools.partial(gather_kernel, n_wide, n_narrow),
        out_shape=[
            jax.ShapeDtypeStruct((groups,) + first.shape, first.dtype),
            jax.ShapeDtypeStruct((n_wide,) + rest.shape, rest.dtype),
        ],
        in_specs=[in_vmem] * 2,
        out_specs=[in_vmem] * 2,
        scratch_shapes=[
            pltpu.SemaphoreType.DMA((2,)),
            pltpu.SemaphoreType.DMA((groups + n_wide,)),
            pltpu.SemaphoreType.DMA((groups + n_wide,)),
        ],
        compiler_params=pltpu.CompilerParams(
            collective_id=0, has_side_effects=True, vmem_limit_bytes=16 * 2**20
        ),
    )(first, rest)


def product(a, b, dims=((1,), (0,))):
    return lax.dot_general(
        a, b, (dims, ((), ())), precision=lax.Precision.HIGHEST, preferred_element_type=jnp.float32
    )


def product_t(a, b):
    return product(a, b, ((1,), (1,)))


def spread_lane(x, lane):
    return jnp.broadcast_to(x[:, lane : lane + 1], x.shape)


def inverse_low_base(block):
    size = block.shape[0]
    rest = block
    done = []
    for g in range(size // 8):
        base = 8 * g
        lane = lax.broadcasted_iota(jnp.int32, (8, size), 1)
        sub = lax.broadcasted_iota(jnp.int32, (8, size), 0)
        rows, rest = rest[:8], rest[8:]
        last = g == size // 8 - 1
        cols = [spread_lane(rows, base + t) for t in range(8)]
        inside = (lane >= base) & (lane < base + 8)
        rows = jnp.where(inside, jnp.where(lane == base + sub, 1.0, 0.0), rows)
        if not last:
            below = [spread_lane(rest, base + t) for t in range(8)]
            lanes = lax.broadcasted_iota(jnp.int32, rest.shape, 1)
            rest = jnp.where((lanes >= base) & (lanes < base + 8), 0.0, rest)
        scale = jnp.zeros((8, size), jnp.float32)
        for t in range(8):
            pivots = [cols[k][t : t + 1, :] for k in range(t, 8)]
            row = rows[t : t + 1, :]
            inv = 1.0 / pivots[0]
            scale = jnp.where(sub == t, lax.rsqrt(pivots[0]), scale)
            factor = jnp.where(sub > t, cols[t] * inv, 0.0)
            rows = rows - factor * row
            for k in range(t + 1, 8):
                cols[k] = cols[k] - factor * pivots[k - t]
            if not last:
                factor = below[t] * inv
                rest = rest - factor * row
                for k in range(t + 1, 8):
                    below[k] = below[k] - factor * pivots[k - t]
        done.append(jnp.where(lane < base + 8, rows, 0.0) * scale)
    return jnp.concatenate(done, axis=0)


def inverse_low(block):
    size = block.shape[0]
    if size <= 128:
        return inverse_low_base(block)
    half = size // 2
    first = inverse_low(block[:half, :half])
    below = product_t(block[half:, :half], first)
    second = inverse_low(block[half:, half:] - product_t(below, below))
    corner = -product(second, product(below, first))
    top = jnp.concatenate([first, jnp.zeros_like(first)], axis=1)
    return jnp.concatenate([top, jnp.concatenate([corner, second], axis=1)], axis=0)


def symmetric(block):
    return 0.5 * (block + block.T)


def bf16_product_t(a, b):
    return lax.dot_general(a, b, (((1,), (1,)), ((), ())), preferred_element_type=jnp.float32)


def two_terms(x):
    high = x.astype(jnp.bfloat16)
    return high, (x - high.astype(jnp.float32)).astype(jnp.bfloat16)


def factor_kernel(strips, panel_ref, metric_ref, weight_ref, high_ref, low_ref, solve_rows):
    strip = DONE // strips
    own = lax.axis_index("narrow")
    weighted = jnp.dot(panel_ref[...], metric_ref[...], preferred_element_type=jnp.float32)
    high, low = two_terms(weighted)
    high_ref[...], low_ref[...] = high, low
    gram = bf16_product_t(panel_ref[:DONE], high) + bf16_product_t(panel_ref[:DONE], low)
    slab = gram * gram

    low0 = inverse_low(symmetric(slab[:PB, :PB]))
    upper = product(low0, slab[:PB, PB:DONE])
    column = product_t(slab[PB:DONE, :PB], low0)
    low1 = inverse_low(symmetric(slab[PB:DONE, PB:DONE] - product(column, upper)))
    zero = jnp.zeros((PB, PB), jnp.float32)
    solves = []
    for cross in (upper.T, column):
        below = jnp.concatenate([-product(low1, product(cross, low0)), low1], axis=1)
        solves.append(jnp.concatenate([jnp.concatenate([low0, zero], axis=1), below], axis=0))
    chunks = []
    for c in range(DONE // 128):
        solve_rows[c] = solves[0][:, c * 128 : (c + 1) * 128]
        picked = solve_rows[c, pl.ds(0, strip, stride=strips), :]
        for s in range(1, strips):
            picked = jnp.where(own == s, solve_rows[c, pl.ds(s, strip, stride=strips), :], picked)
        chunks.append(picked)
    weight_ref[:, :strip] = jnp.concatenate(chunks, axis=1).T
    weight_ref[:, strip:] = product(solves[0], product(solves[1], slab[:, DONE:]), ((0,), (0,)))


def factor(panel, metric, strips):
    in_vmem = pl.BlockSpec(memory_space=pltpu.VMEM)
    terms = jax.ShapeDtypeStruct(panel.shape, jnp.bfloat16)
    width = P_SIZE // strips
    flops = 2 * panel.shape[0] * panel.shape[1] * metric.shape[0] * 20
    return pl.pallas_call(
        functools.partial(factor_kernel, strips),
        out_shape=[jax.ShapeDtypeStruct((DONE, width), jnp.float32), terms, terms],
        in_specs=[in_vmem] * 2,
        out_specs=[in_vmem] * 3,
        scratch_shapes=[pltpu.VMEM((DONE // 128, DONE, 128), jnp.float32)],
        compiler_params=pltpu.CompilerParams(vmem_limit_bytes=48 * 2**20),
        cost_estimate=pl.CostEstimate(flops=flops, bytes_accessed=2**22, transcendentals=0),
    )(panel, metric)


def finish_kernel(rows_ref, high_ref, low_ref, weight_ref, out_ref):
    strips, row_count, order = rows_ref.shape
    strip = DONE // strips
    rows = rows_ref[...].reshape(strips * row_count, order)
    gram = bf16_product_t(rows, high_ref[...]) + bf16_product_t(rows, low_ref[...])
    slab = gram * gram
    solved = product(slab[:, :DONE], weight_ref[...])
    for s in range(strips):
        part = slice(s * row_count, (s + 1) * row_count)
        trailing = slab[part, DONE:] - solved[part, strip:]
        out_ref[:, s] = jnp.concatenate([solved[part, :strip], trailing], axis=1)[:, None, :]


def finish(rows, high, low, weight):
    strips, row_count, order = rows.shape
    width = weight.shape[1]
    block = 128
    whole = lambda x: pl.BlockSpec(x.shape, lambda i: (0, 0))
    return pl.pallas_call(
        finish_kernel,
        out_shape=jax.ShapeDtypeStruct((row_count, strips, 1, width), jnp.float32),
        grid=(row_count // block,),
        in_specs=[
            pl.BlockSpec((strips, block, order), lambda i: (0, i, 0)),
            whole(high),
            whole(low),
            whole(weight),
        ],
        out_specs=pl.BlockSpec((block, strips, 1, width), lambda i: (i, 0, 0, 0)),
        compiler_params=pltpu.CompilerParams(vmem_limit_bytes=48 * 2**20),
    )(rows, high, low, weight)


def local(constraint_rows, metric):
    n_wide, strips = lax.axis_size("wide"), lax.axis_size("narrow")
    groups = n_wide * strips
    depth = P_SIZE // groups
    ahead = DONE // groups
    order = metric.shape[0]
    own_rows = constraint_rows[:, 0, :]
    rows = lax.all_gather(own_rows, "narrow", axis=0, tiled=False)
    firsts, rests = gather_panel(own_rows[:ahead], own_rows[ahead:depth], n_wide, strips)
    first = firsts.transpose(1, 0, 2).reshape(DONE, order)
    rest = rests.transpose(1, 0, 2).reshape((P_SIZE - DONE) // strips, order)
    weight, high, low = factor(jnp.concatenate([first, rest], axis=0), metric, strips)
    return finish(rows, high, low, weight)


def solution(mesh):
    placed = (P(None, ("wide", "narrow"), None), P())
    return jax.shard_map(
        local,
        mesh=mesh,
        in_specs=placed,
        out_specs=P(None, "wide", "narrow", None),
        check_vma=False,
    )
```

time: 97.1 us -> 117 us (1.20)
  waiting for transfers between devices: 0 us -> 38.8 us
  blocking collectives: 29.8 us -> 0 us
  Pallas kernels: 47.8 us -> 62.5 us
  between operations: 0.04 us -> 13.4 us
  local copies, waits for them, and re-layouts: 10.4 us -> 1.51 us
  matrix products: 8.6 us -> 0 us
    all_gather x0 -> x1, waiting for transfers between devices: none -> 38.1 us  [local(): rows = lax.all_gather(own_rows, 'narrow', axis=0, tiled=False)]
    all_to_all x1 -> x0, blocking collectives: 29.8 us -> none  [local(): lax.all_to_all(strips_out, 'narrow', split_axis=0, concat_axis=0, tiled=T...]
    pallas_call x1 -> x2, Pallas kernels: 25.6 us -> 45.1 us  [the longest x1 28.1 us: factor(): pl.pallas_call(functools.partial(factor_kernel, strips), out_shape=[jax.S...]
    dot_general x1 -> x0, matrix products: 8.6 us -> none  [local(): lax.dot_general(projected, panel, (((1,), (1,)), ((), ())), preferred_ele...]
    pallas_call x1, Pallas kernels: 22.2 us -> 17.3 us  [gather_panel(): pl.pallas_call(functools.partial(gather_kernel, n_wide, n_narrow), out_sh...]
    broadcast_in_dim x1 -> x0, local copies, waits for them, and re-layouts: 3.48 us -> none  [local(): return mine.astype(jnp.float32).transpose(1, 0, 2)[:, :, None, :]]
    unnamed x4 -> x0, local copies, waits for them, and re-layouts: 2.19 us -> none
    transpose x3 -> x2, local copies, waits for them, and re-layouts: 2.68 us -> 0.73 us  [the longest x1 0.58 us: local(): first = firsts.transpose(1, 0, 2).reshape(DONE, order)]
  transfers between devices with their start and end apart: 0 -> 1, of which waited for: 0 -> 1; matrix products, arithmetic and copies ran while one was open for 0% -> 1% of each run, Pallas kernels for 0% -> 39%
where the time goes in v2:
time: 117 us; the launch traced here: 116 us
  Pallas kernels  62.5 us (53%)
  waiting for transfers between devices  38.8 us (33%)
  between operations  13.4 us (11%)
  local copies, waits for them, and re-layouts  1.51 us (1%)
    all_gather x1, waiting for transfers between devices, local(): rows = lax.all_gather(own_rows, 'narrow', axis=0, tiled=False)  38.1 us
    pallas_call x1, Pallas kernels, factor(): pl.pallas_call(functools.partial(factor_kernel, strips), out_shape=[jax.S...  28.1 us
    pallas_call x1, Pallas kernels, gather_panel(): pl.pallas_call(functools.partial(gather_kernel, n_wide, n_narrow), out_sh...  17.3 us
    pallas_call x1, Pallas kernels, finish(): pl.pallas_call(finish_kernel, out_shape=jax.ShapeDtypeStruct((row_count,...  17.1 us
  transfers between devices with their start and end apart: 1, of which 1 were waited for; matrix products, arithmetic and copies ran while one was open for 1% of the time, Pallas kernels for 39%

profile of v2, /device:TPU:0, one launch (start us, length us, event | category | flops | bytes accessed | tf_op | source)
XLA Modules:
  0.0 116.3 jit_solution(11706913177946813601)
XLA Ops:
  6.5 0.0 all-gather.3.cloned.1.call-start
  6.5 0.7 all-gather.3.cloned.1.call-update
  7.3 0.8 slice_bitcast_fusion
  8.0 17.3 %shard_map.28 = (bf16[32,16,1024]{2,1,0:T(8,128)(2,1)S(1)}, bf16[8,16,1024]{2,1,0:T(8,128)(2,1)S(1)}) custom-call(bf16[16,1024]{1,0:T(8,128)(2,1)S(1)} %get-tuple-element.16.first_ref, bf16[16,1024]{1,0:T(8,128)(2,1)S(1)} %get-tuple-element.15.rest_ref), custom_call_target="tpu_custom_call" | custom-call | tf_op jit(solution)/shard_map/pallas_call | solution.py:97
  25.4 0.6 copy.3
  26.0 0.2 copy.6
  26.1 0.1 pad_maximum_fusion.panel_ref
  26.2 28.1 %shard_map.29 = (f32[512,256]{1,0:T(8,128)S(1)}, bf16[640,1024]{1,0:T(8,128)(2,1)S(1)}, bf16[640,1024]{1,0:T(8,128)(2,1)S(1)}) custom-call(bf16[640,1024]{1,0:T(8,128)(2,1)S(1)} %pad_maximum_fusion.panel_ref, bf16[1024,1024]{1,0:T(8,128)(2,1)} %metric_ref.1), custom_call_target="tpu_custom_call" | custom-call | flops 26843545600 | bytes 4194304 | tf_op jit(solution)/shard_map/pallas_call | solution.py:226
  54.3 38.1 %all-gather.3.cloned.1.call-done = bf16[2048,1,1024]{2,0,1:T(8,128)(2,1)} async-done(((bf16[512,1,1024]{2,0,1:T(8,128)(2,1)}), bf16[2048,1,1024]{2,0,1:T(8,128)(2,1)}) %all-gather.3.cloned.1.call-update) | async-done | bytes 4194320 | tf_op jit(solution)/shard_map/all_gather | solution.py:277
  92.4 17.1 %shard_map.30 = f32[512,4,1,256]{3,2,1,0:T(1,128)} custom-call(bf16[4,512,1024]{2,1,0:T(8,128)(2,1)} %bitcast.13, bf16[640,1024]{1,0:T(8,128)(2,1)S(1)} %get-tuple-element.12.high_ref, bf16[640,1024]{1,0:T(8,128)(2,1)S(1)} %get-tuple-element.13.low_ref, f32[512,256]{1,0:T(8,128)S(1)} %get-tuple-element.14.weight_ref), custom_call_target="tpu_custom_call" | custom-call | tf_op jit(solution)/shard_map/pallas_call | solution.py:255
Async XLA Ops:
  6.5 85.9 %all-gather.3.cloned.1.call-start = ((), (), s32[]{:S(2)}) async-start(), calls=%async_computation | async-start | bytes 5242880 | tf_op jit(solution)/shard_map/all_gather | solution.py:277
Sparse Core Ops, SparseCore 0:
  8.9 83.4 all-gather.2

commit v3 on v1

--- a/solution.py
+++ b/solution.py
@@ -109,40 +109,40 @@
     return jnp.broadcast_to(x[:, lane : lane + 1], x.shape)
 
 
-def spread_row(x, row):
-    return jnp.broadcast_to(x[row : row + 1, :], x.shape)
-
-
 def inverse_low_base(block):
     size = block.shape[0]
-    tiles = [block[8 * g : 8 * g + 8, :] for g in range(size // 8)]
-    lane = lax.broadcasted_iota(jnp.int32, (8, size), 1)
-    sub = lax.broadcasted_iota(jnp.int32, (8, size), 0)
+    rest = block
+    done = []
     for g in range(size // 8):
         base = 8 * g
+        lane = lax.broadcasted_iota(jnp.int32, (8, size), 1)
+        sub = lax.broadcasted_iota(jnp.int32, (8, size), 0)
+        rows, rest = rest[:8], rest[8:]
+        last = g == size // 8 - 1
+        cols = [spread_lane(rows, base + t) for t in range(8)]
         inside = (lane >= base) & (lane < base + 8)
-        later = range(g + 1, size // 8)
-        cols = {h: [spread_lane(tiles[h], base + t) for t in range(8)] for h in [g, *later]}
-        rows = jnp.where(inside, jnp.where(lane == base + sub, 1.0, 0.0), tiles[g])
-        for h in later:
-            tiles[h] = jnp.where(inside, 0.0, tiles[h])
+        rows = jnp.where(inside, jnp.where(lane == base + sub, 1.0, 0.0), rows)
+        if not last:
+            below = [spread_lane(rest, base + t) for t in range(8)]
+            lanes = lax.broadcasted_iota(jnp.int32, rest.shape, 1)
+            rest = jnp.where((lanes >= base) & (lanes < base + 8), 0.0, rest)
         scale = jnp.zeros((8, size), jnp.float32)
         for t in range(8):
-            pivots = [spread_row(cols[g][k], t) for k in range(t, 8)]
-            row = spread_row(rows, t)
+            pivots = [cols[k][t : t + 1, :] for k in range(t, 8)]
+            row = rows[t : t + 1, :]
             inv = 1.0 / pivots[0]
             scale = jnp.where(sub == t, lax.rsqrt(pivots[0]), scale)
-            factor = jnp.where(sub > t, cols[g][t] * inv, 0.0)
+            factor = jnp.where(sub > t, cols[t] * inv, 0.0)
             rows = rows - factor * row
             for k in range(t + 1, 8):
-                cols[g][k] = cols[g][k] - factor * pivots[k - t]
-            for h in later:
-                factor = cols[h][t] * inv
-                tiles[h] = tiles[h] - factor * row
+                cols[k] = cols[k] - factor * pivots[k - t]
+            if not last:
+                factor = below[t] * inv
+                rest = rest - factor * row
                 for k in range(t + 1, 8):
-                    cols[h][k] = cols[h][k] - factor * pivots[k - t]
-        tiles[g] = jnp.where(lane < base + 8, rows, 0.0) * scale
-    return jnp.concatenate(tiles, axis=0)
+                    below[k] = below[k] - factor * pivots[k - t]
+        done.append(jnp.where(lane < base + 8, rows, 0.0) * scale)
+    return jnp.concatenate(done, axis=0)
 
 
 def inverse_low(block):
@@ -162,64 +162,151 @@
     return 0.5 * (block + block.T)
 
 
-def factor_kernel(strips, slab_ref, out_ref, solve_rows, solve_cols):
+def bf16_product_t(a, b):
+    return lax.dot_general(a, b, (((1,), (1,)), ((), ())), preferred_element_type=jnp.float32)
+
+
+def two_terms(x):
+    high = x.astype(jnp.bfloat16)
+    return high, (x - high.astype(jnp.float32)).astype(jnp.bfloat16)
+
+
+def factor_kernel(strips, panel_ref, metric_ref, solve_ref, upper_ref, high_ref, low_ref, chunk_ref):
     strip = DONE // strips
-    low0 = inverse_low(symmetric(slab_ref[:PB, :PB]))
-    upper = product(low0, slab_ref[:PB, PB:DONE])
-    column = product_t(slab_ref[PB:DONE, :PB], low0)
-    low1 = inverse_low(symmetric(slab_ref[PB:DONE, PB:DONE] - product(column, upper)))
+    weighted = jnp.dot(panel_ref[...], metric_ref[...], preferred_element_type=jnp.float32)
+    high, low = two_terms(weighted)
+    high_ref[...], low_ref[...] = high, low
+    gram = bf16_product_t(panel_ref[:DONE], high) + bf16_product_t(panel_ref[:DONE], low)
+    slab = gram * gram
+
+    low0 = inverse_low(symmetric(slab[:PB, :PB]))
+    upper = product(low0, slab[:PB, PB:DONE])
+    column = product_t(slab[PB:DONE, :PB], low0)
+    low1 = inverse_low(symmetric(slab[PB:DONE, PB:DONE] - product(column, upper)))
     zero = jnp.zeros((PB, PB), jnp.float32)
     by_strip = []
-    for ref, cross in ((solve_rows, upper.T), (solve_cols, column)):
+    for which, cross in enumerate((upper.T, column)):
         below = jnp.concatenate([-product(low1, product(cross, low0)), low1], axis=1)
         solve = jnp.concatenate([jnp.concatenate([low0, zero], axis=1), below], axis=0)
-        for c in range(DONE // 128):
-            ref[c] = solve[:, c * 128 : (c + 1) * 128]
         chunks = []
         for c in range(DONE // 128):
-            picked = [ref[c, pl.ds(s, strip, stride=strips), :] for s in range(strips)]
+            chunk_ref[which, c] = solve[:, c * 128 : (c + 1) * 128]
+            picked = [chunk_ref[which, c, pl.ds(s, strip, stride=strips), :] for s in range(strips)]
             chunks.append(jnp.concatenate(picked, axis=0))
         by_strip.append(jnp.concatenate(chunks, axis=1))
-    upper_all = product(by_strip[1], slab_ref[:DONE, DONE:])
-    columns = product_t(slab_ref[DONE:, :DONE], by_strip[0])
-    trailing = slab_ref[DONE:, DONE:] - product(columns, upper_all)
-    for s in range(strips):
-        cut = slice(s * strip, (s + 1) * strip)
-        out_ref[s, :, :strip] = columns[:, cut].astype(out_ref.dtype)
-        out_ref[s, :, strip:] = trailing[:, cut].astype(out_ref.dtype)
-
-
-def factor(slab, strips):
-    row_count = slab.shape[0] - DONE
+    solve_ref[...] = by_strip[0]
+    upper_ref[...] = product(by_strip[1], slab[:, DONE:])
+
+
+def factor(panel, metric, strips):
+    in_vmem = pl.BlockSpec(memory_space=pltpu.VMEM)
+    terms = jax.ShapeDtypeStruct(panel.shape, jnp.bfloat16)
     return pl.pallas_call(
         functools.partial(factor_kernel, strips),
-        out_shape=jax.ShapeDtypeStruct((strips, row_count, P_SIZE // strips), jnp.bfloat16),
-        in_specs=[pl.BlockSpec(memory_space=pltpu.VMEM)],
-        out_specs=pl.BlockSpec(memory_space=pltpu.VMEM),
-        scratch_shapes=[pltpu.VMEM((DONE // 128, DONE, 128), jnp.float32)] * 2,
+        out_shape=[
+            jax.ShapeDtypeStruct((DONE, DONE), jnp.float32),
+            jax.ShapeDtypeStruct((DONE, P_SIZE - DONE), jnp.float32),
+            terms,
+            terms,
+        ],
+        in_specs=[in_vmem] * 2,
+        out_specs=[in_vmem] * 4,
+        scratch_shapes=[pltpu.VMEM((2, DONE // 128, DONE, 128), jnp.float32)],
         compiler_params=pltpu.CompilerParams(vmem_limit_bytes=48 * 2**20),
-    )(slab)
+    )(panel, metric)
+
+
+def finish_kernel(
+    strips, chunks, rows_ref, high_ref, low_ref, solve_ref, upper_ref, out_ref, made, own_sem, send_sem, recv_sem
+):
+    w, z = lax.axis_index("wide"), lax.axis_index("narrow")
+    column = [lax.rem(z + i, strips) for i in range(1, strips)]
+    strip = DONE // strips
+    block = rows_ref.shape[0] // chunks
+    barrier = pltpu.get_barrier_semaphore()
+    for p in column:
+        pl.semaphore_signal(barrier, inc=1, device_id=(w, p), device_id_type=MESH)
+
+    copies, kept = [], []
+    for c in range(chunks):
+        part = pl.ds(c * block, block)
+        rows = rows_ref[part, :]
+        gram = bf16_product_t(rows, high_ref[...]) + bf16_product_t(rows, low_ref[...])
+        slab = gram * gram
+        solved = product_t(slab[:, :DONE], solve_ref[...])
+        trailing = slab[:, DONE:] - product(solved, upper_ref[...])
+        for s in range(strips):
+            cut = slice(s * strip, (s + 1) * strip)
+            both = jnp.concatenate([solved[:, cut], trailing[:, cut]], axis=1)
+            made[s, part, :] = both.astype(made.dtype)
+        if c == 0:
+            pl.semaphore_wait(barrier, strips - 1)
+        for i, p in enumerate(column):
+            copy = pltpu.make_async_remote_copy(
+                src_ref=made.at[p, part],
+                dst_ref=out_ref.at[z, part],
+                send_sem=send_sem.at[c, i],
+                recv_sem=recv_sem.at[c, z],
+                device_id=(w, p),
+                device_id_type=MESH,
+            )
+            copy.start()
+            copies.append(copy)
+        keep = pltpu.make_async_copy(made.at[z, part], out_ref.at[z, part], own_sem.at[c])
+        keep.start()
+        kept.append(keep)
+    for c in range(chunks):
+        part = pl.ds(c * block, block)
+        for p in column:
+            pltpu.make_async_remote_copy(
+                src_ref=made.at[p, part],
+                dst_ref=out_ref.at[p, part],
+                send_sem=send_sem.at[c, 0],
+                recv_sem=recv_sem.at[c, p],
+                device_id=(w, p),
+                device_id_type=MESH,
+            ).wait_recv()
+        kept[c].wait()
+    for copy in copies:
+        copy.wait_send()
+
+
+def finish(rows, high, low, solve, upper, strips):
+    row_count = rows.shape[0]
+    chunks = 4
+    in_vmem = pl.BlockSpec(memory_space=pltpu.VMEM)
+    out = jax.ShapeDtypeStruct((strips, row_count, P_SIZE // strips), jnp.bfloat16)
+    return pl.pallas_call(
+        functools.partial(finish_kernel, strips, chunks),
+        out_shape=out,
+        in_specs=[in_vmem] * 5,
+        out_specs=in_vmem,
+        scratch_shapes=[
+            pltpu.VMEM(out.shape, out.dtype),
+            pltpu.SemaphoreType.DMA((chunks,)),
+            pltpu.SemaphoreType.DMA((chunks, strips - 1)),
+            pltpu.SemaphoreType.DMA((chunks, strips)),
+        ],
+        compiler_params=pltpu.CompilerParams(
+            collective_id=1, has_side_effects=True, vmem_limit_bytes=48 * 2**20
+        ),
+    )(rows, high, low, solve, upper)
 
 
 def local(constraint_rows, metric):
     n_wide, strips = lax.axis_size("wide"), lax.axis_size("narrow")
     groups = n_wide * strips
     depth = P_SIZE // groups
+    ahead = DONE // groups
     order = metric.shape[0]
     own_rows = constraint_rows[:, 0, :]
     gathered = gather_panel(own_rows[:depth], n_wide, strips)
     gathered = gathered.reshape(n_wide, strips, depth, order)
-    ahead = DONE // groups
     first = gathered[:, :, :ahead].transpose(2, 0, 1, 3).reshape(DONE, order)
     rest = gathered[:, :, ahead:].transpose(1, 2, 0, 3).reshape(P_SIZE - DONE, order)
     panel = jnp.concatenate([first, rest], axis=0)
-    rows = jnp.concatenate([first, own_rows], axis=0)
-    projected = jnp.dot(rows, metric, preferred_element_type=jnp.float32).astype(jnp.bfloat16)
-    gram = lax.dot_general(
-        projected, panel, (((1,), (1,)), ((), ())), preferred_element_type=jnp.float32
-    )
-    strips_out = factor(gram * gram, strips)
-    mine = lax.all_to_all(strips_out, "narrow", split_axis=0, concat_axis=0, tiled=True)
+    solve, upper, high, low = factor(panel, metric, strips)
+    mine = finish(own_rows, high, low, solve, upper, strips)
     return mine.astype(jnp.float32).transpose(1, 0, 2)[:, :, None, :]
 
 

time: 97.1 us -> 89.2 us (0.919)
  Pallas kernels: 47.8 us -> 79.6 us
  blocking collectives: 29.8 us -> 0 us
  matrix products: 8.6 us -> 0 us
  local copies, waits for them, and re-layouts: 10.4 us -> 7.54 us
  other arithmetic: 0.18 us -> 1.77 us
    pallas_call x1 -> x2, Pallas kernels: 25.6 us -> 57.4 us  [the longest x1 29.3 us: finish(): pl.pallas_call(functools.partial(finish_kernel, strips, chunks), out_shap...]
    all_to_all x1 -> x0, blocking collectives: 29.8 us -> none  [local(): lax.all_to_all(strips_out, 'narrow', split_axis=0, concat_axis=0, tiled=T...]
    dot_general x1 -> x0, matrix products: 8.6 us -> none  [local(): lax.dot_general(projected, panel, (((1,), (1,)), ((), ())), preferred_ele...]
    transpose x3 -> x0, local copies, waits for them, and re-layouts: 2.68 us -> none  [the longest x2 1.87 us: local(): gathered[:, :, ahead:].transpose(1, 2, 0, 3).reshape(P_SIZE - DONE, order)]
    concatenate x0 -> x1, other arithmetic: none -> 1.59 us  [local(): panel = jnp.concatenate([first, rest], axis=0)]
    unnamed x4 -> x6, local copies, waits for them, and re-layouts: 2.19 us -> 2.71 us
where the time goes in v3:
time: 89.2 us; the launch traced here: 89 us
  Pallas kernels  79.6 us (89%)
  local copies, waits for them, and re-layouts  7.54 us (8%)
  other arithmetic  1.77 us (2%)
    pallas_call x1, Pallas kernels, finish(): pl.pallas_call(functools.partial(finish_kernel, strips, chunks), out_shap...  29.3 us
    pallas_call x1, Pallas kernels, factor(): pl.pallas_call(functools.partial(factor_kernel, strips), out_shape=[jax.S...  28.1 us
    pallas_call x1, Pallas kernels, gather_panel(): pl.pallas_call(functools.partial(gather_kernel, n_wide, n_narrow), out_sh...  22.2 us
    broadcast_in_dim x1, local copies, waits for them, and re-layouts, local(): return mine.astype(jnp.float32).transpose(1, 0, 2)[:, :, None, :]  3.48 us
    unnamed x6, local copies, waits for them, and re-layouts  2.71 us

profile of v3, /device:TPU:0, one launch (start us, length us, event | category | flops | bytes accessed | tf_op | source)
XLA Modules:
  0.0 89.0 jit_solution(15727340869029113291)
XLA Ops:
  0.0 0.8 slice_bitcast_fusion.own_ref
  0.8 22.2 %shard_map.28 = bf16[32,32,1024]{2,1,0:T(8,128)(2,1)S(1)} custom-call(bf16[32,1024]{1,0:T(8,128)(2,1)S(1)} %slice_bitcast_fusion.own_ref), custom_call_target="tpu_custom_call" | custom-call | tf_op jit(solution)/shard_map/pallas_call | solution.py:82
  23.1 0.2 fusion
  23.3 0.8 copy.9
  24.1 0.3 reshape.11
  24.4 0.6 copy.7
  25.0 1.6 %pad_maximum_fusion.panel_ref = bf16[1024,1024]{1,0:T(8,128)(2,1)} fusion(bf16[512,1024]{1,0:T(8,128)(2,1)S(1)} %bitcast.17, bf16[512,1024]{1,0:T(8,128)(2,1)S(1)} %reshape.11), kind=kLoop, calls=%fused_computation | loop fusion | flops 4194304 | bytes 4194304 | tf_op jit(solution)/shard_map/concatenate | solution.py:307
  26.6 0.0 copy-start.1
  26.6 28.1 %shard_map.29 = (f32[512,512]{1,0:T(8,128)S(1)}, f32[512,512]{1,0:T(8,128)S(1)}, bf16[1024,1024]{1,0:T(8,128)(2,1)S(1)}, bf16[1024,1024]{1,0:T(8,128)(2,1)}) custom-call(bf16[1024,1024]{1,0:T(8,128)(2,1)} %pad_maximum_fusion.panel_ref, bf16[1024,1024]{1,0:T(8,128)(2,1)} %metric_ref.1), custom_call_target="tpu_custom_call" | custom-call | tf_op jit(solution)/shard_map/pallas_call | solution.py:204
  54.7 0.0 copy-start
  54.7 1.3 %copy-done = bf16[1024,1024]{1,0:T(8,128)(2,1)} copy-done((bf16[1024,1024]{1,0:T(8,128)(2,1)}, bf16[1024,1024]{1,0:T(8,128)(2,1)S(1)}, u32[]{:S(2)}) %copy-start) | copy-done | bytes 2097176
  56.0 0.0 copy-done.1
  56.0 29.3 %shard_map.30 = bf16[4,512,256]{2,1,0:T(8,128)(2,1)S(1)} custom-call(bf16[512,1024]{1,0:T(8,128)(2,1)S(1)} %bitcast.15, bf16[1024,1024]{1,0:T(8,128)(2,1)} %copy-done, bf16[1024,1024]{1,0:T(8,128)(2,1)} %get-tuple-element.10.low_ref, f32[512,512]{1,0:T(8,128)S(1)} %get-tuple-element.11.solve_ref, f32[512,512]{1,0:T(8,128)S(1)} %get-tuple-element.12.upper_ref), custom_call_target="tpu_custom_call" | custom-call | tf_op jit(solution)/shard_map/pallas_call | solution.py:279
  85.3 0.2 convert_bitcast_fusion
  85.5 3.5 %copy.5 = f32[512,4,1,256]{3,2,1,0:T(1,128)} copy(f32[512,4,1,256]{3,0,1,2:T(8,128)S(1)} %convert_bitcast_fusion) | data formatting | bytes 4194304 | tf_op jit(solution)/shard_map/broadcast_in_dim | solution.py:310
Async XLA Ops:
  26.6 29.4 %copy-start.1 = (bf16[512,1,1024]{2,0,1:T(8,128)(2,1)S(1)}, bf16[512,1,1024]{2,0,1:T(8,128)(2,1)}, u32[]{:S(2)}) copy-start(bf16[512,1,1024]{2,0,1:T(8,128)(2,1)} %param.2) | copy-start | bytes 3145732
  54.7 1.3 %copy-start = (bf16[1024,1024]{1,0:T(8,128)(2,1)}, bf16[1024,1024]{1,0:T(8,128)(2,1)S(1)}, u32[]{:S(2)}) copy-start(bf16[1024,1024]{1,0:T(8,128)(2,1)S(1)} %get-tuple-element.9.high_ref) | copy-start | bytes 6291460

commit v4 on v3

--- a/solution.py
+++ b/solution.py
@@ -171,7 +171,7 @@
     return high, (x - high.astype(jnp.float32)).astype(jnp.bfloat16)
 
 
-def factor_kernel(strips, panel_ref, metric_ref, solve_ref, upper_ref, high_ref, low_ref, chunk_ref):
+def factor_kernel(strips, panel_ref, metric_ref, solve_ref, upper_ref, weight_ref, high_ref, low_ref, chunk_ref):
     strip = DONE // strips
     weighted = jnp.dot(panel_ref[...], metric_ref[...], preferred_element_type=jnp.float32)
     high, low = two_terms(weighted)
@@ -195,7 +195,17 @@
             chunks.append(jnp.concatenate(picked, axis=0))
         by_strip.append(jnp.concatenate(chunks, axis=1))
     solve_ref[...] = by_strip[0]
-    upper_ref[...] = product(by_strip[1], slab[:, DONE:])
+    upper_all = product(by_strip[1], slab[:, DONE:])
+    upper_ref[...] = upper_all
+
+    own = lax.axis_index("narrow")
+    solve_own, upper_own = by_strip[0][:strip], upper_all[:, :strip]
+    for s in range(1, strips):
+        cut = slice(s * strip, (s + 1) * strip)
+        solve_own = jnp.where(own == s, by_strip[0][cut], solve_own)
+        upper_own = jnp.where(own == s, upper_all[:, cut], upper_own)
+    weight_ref[:, :strip] = solve_own.T
+    weight_ref[:, strip:] = product(by_strip[0], upper_own, ((0,), (0,)))
 
 
 def factor(panel, metric, strips):
@@ -206,31 +216,36 @@
         out_shape=[
             jax.ShapeDtypeStruct((DONE, DONE), jnp.float32),
             jax.ShapeDtypeStruct((DONE, P_SIZE - DONE), jnp.float32),
+            jax.ShapeDtypeStruct((DONE, P_SIZE // strips), jnp.float32),
             terms,
             terms,
         ],
         in_specs=[in_vmem] * 2,
-        out_specs=[in_vmem] * 4,
+        out_specs=[in_vmem] * 5,
         scratch_shapes=[pltpu.VMEM((2, DONE // 128, DONE, 128), jnp.float32)],
         compiler_params=pltpu.CompilerParams(vmem_limit_bytes=48 * 2**20),
     )(panel, metric)
 
 
 def finish_kernel(
-    strips, chunks, rows_ref, high_ref, low_ref, solve_ref, upper_ref, out_ref, made, own_sem, send_sem, recv_sem
+    strips, chunks, rows_ref, near_ref, high_ref, low_ref, solve_ref, upper_ref, weight_ref,
+    out_ref, made, near, near_sem, own_sem, send_sem, recv_sem,
 ):
     w, z = lax.axis_index("wide"), lax.axis_index("narrow")
     column = [lax.rem(z + i, strips) for i in range(1, strips)]
     strip = DONE // strips
+    gathered = near_ref.shape[1]
     block = rows_ref.shape[0] // chunks
+    fetch = pltpu.make_async_copy(near_ref, near, near_sem)
+    fetch.start()
     barrier = pltpu.get_barrier_semaphore()
     for p in column:
         pl.semaphore_signal(barrier, inc=1, device_id=(w, p), device_id_type=MESH)
 
     copies, kept = [], []
     for c in range(chunks):
-        part = pl.ds(c * block, block)
-        rows = rows_ref[part, :]
+        part = pl.ds(gathered + c * block, block)
+        rows = rows_ref[pl.ds(c * block, block), :]
         gram = bf16_product_t(rows, high_ref[...]) + bf16_product_t(rows, low_ref[...])
         slab = gram * gram
         solved = product_t(slab[:, :DONE], solve_ref[...])
@@ -238,12 +253,12 @@
         for s in range(strips):
             cut = slice(s * strip, (s + 1) * strip)
             both = jnp.concatenate([solved[:, cut], trailing[:, cut]], axis=1)
-            made[s, part, :] = both.astype(made.dtype)
+            made[s, pl.ds(c * block, block), :] = both.astype(made.dtype)
         if c == 0:
             pl.semaphore_wait(barrier, strips - 1)
         for i, p in enumerate(column):
             copy = pltpu.make_async_remote_copy(
-                src_ref=made.at[p, part],
+                src_ref=made.at[p, pl.ds(c * block, block)],
                 dst_ref=out_ref.at[z, part],
                 send_sem=send_sem.at[c, i],
                 recv_sem=recv_sem.at[c, z],
@@ -252,14 +267,25 @@
             )
             copy.start()
             copies.append(copy)
-        keep = pltpu.make_async_copy(made.at[z, part], out_ref.at[z, part], own_sem.at[c])
+        keep = pltpu.make_async_copy(made.at[z, pl.ds(c * block, block)], out_ref.at[z, part], own_sem.at[c])
         keep.start()
         kept.append(keep)
+
+    fetch.wait()
+    own_rows = pl.ds(pl.multiple_of(DONE + z * strip, 16), strip)
+    for n in range(strips):
+        rows = near[n]
+        gram = bf16_product_t(rows, high_ref[:DONE]) + bf16_product_t(rows, low_ref[:DONE])
+        solved = product(gram * gram, weight_ref[...])
+        gram = bf16_product_t(rows, high_ref[own_rows, :]) + bf16_product_t(rows, low_ref[own_rows, :])
+        both = jnp.concatenate([solved[:, :strip], gram * gram - solved[:, strip:]], axis=1)
+        out_ref[n, pl.ds(0, gathered), :] = both.astype(out_ref.dtype)
+
     for c in range(chunks):
-        part = pl.ds(c * block, block)
+        part = pl.ds(gathered + c * block, block)
         for p in column:
             pltpu.make_async_remote_copy(
-                src_ref=made.at[p, part],
+                src_ref=made.at[p, pl.ds(c * block, block)],
                 dst_ref=out_ref.at[p, part],
                 send_sem=send_sem.at[c, 0],
                 recv_sem=recv_sem.at[c, p],
@@ -271,18 +297,21 @@
         copy.wait_send()
 
 
-def finish(rows, high, low, solve, upper, strips):
+def finish(rows, near, high, low, solve, upper, weight):
+    strips, gathered, order = near.shape
     row_count = rows.shape[0]
-    chunks = 4
+    chunks = 2
     in_vmem = pl.BlockSpec(memory_space=pltpu.VMEM)
-    out = jax.ShapeDtypeStruct((strips, row_count, P_SIZE // strips), jnp.bfloat16)
+    width = P_SIZE // strips
     return pl.pallas_call(
         functools.partial(finish_kernel, strips, chunks),
-        out_shape=out,
-        in_specs=[in_vmem] * 5,
+        out_shape=jax.ShapeDtypeStruct((strips, gathered + row_count, width), jnp.bfloat16),
+        in_specs=[in_vmem, pl.BlockSpec(memory_space=pl.ANY)] + [in_vmem] * 5,
         out_specs=in_vmem,
         scratch_shapes=[
-            pltpu.VMEM(out.shape, out.dtype),
+            pltpu.VMEM((strips, row_count, width), jnp.bfloat16),
+            pltpu.VMEM(near.shape, near.dtype),
+            pltpu.SemaphoreType.DMA,
             pltpu.SemaphoreType.DMA((chunks,)),
             pltpu.SemaphoreType.DMA((chunks, strips - 1)),
             pltpu.SemaphoreType.DMA((chunks, strips)),
@@ -290,7 +319,7 @@
         compiler_params=pltpu.CompilerParams(
             collective_id=1, has_side_effects=True, vmem_limit_bytes=48 * 2**20
         ),
-    )(rows, high, low, solve, upper)
+    )(rows, near, high, low, solve, upper, weight)
 
 
 def local(constraint_rows, metric):
@@ -300,13 +329,15 @@
     ahead = DONE // groups
     order = metric.shape[0]
     own_rows = constraint_rows[:, 0, :]
+    half = own_rows.shape[0] // 2
+    near = lax.all_gather(own_rows[:half], "narrow", axis=0, tiled=False)
     gathered = gather_panel(own_rows[:depth], n_wide, strips)
     gathered = gathered.reshape(n_wide, strips, depth, order)
     first = gathered[:, :, :ahead].transpose(2, 0, 1, 3).reshape(DONE, order)
     rest = gathered[:, :, ahead:].transpose(1, 2, 0, 3).reshape(P_SIZE - DONE, order)
     panel = jnp.concatenate([first, rest], axis=0)
-    solve, upper, high, low = factor(panel, metric, strips)
-    mine = finish(own_rows, high, low, solve, upper, strips)
+    solve, upper, weight, high, low = factor(panel, metric, strips)
+    mine = finish(own_rows[half:], near, high, low, solve, upper, weight)
     return mine.astype(jnp.float32).transpose(1, 0, 2)[:, :, None, :]
 
 

time: 89.2 us -> 96.7 us (1.084)
  between operations: 0.07 us -> 13.4 us
  Pallas kernels: 79.6 us -> 70.2 us
  local copies, waits for them, and re-layouts: 7.54 us -> 11.1 us
    pallas_call x1, Pallas kernels: 29.3 us -> 18.2 us  [finish(): pl.pallas_call(functools.partial(finish_kernel, strips, chunks), out_shap...]
    slice x0 -> x1, local copies, waits for them, and re-layouts: none -> 2.07 us  [local(): near = lax.all_gather(own_rows[:half], 'narrow', axis=0, tiled=False)]
    pallas_call x1, Pallas kernels: 28.1 us -> 29.8 us  [factor(): pl.pallas_call(functools.partial(factor_kernel, strips), out_shape=[jax.S...]
  transfers between devices with their start and end apart: 0 -> 1, of which waited for: 0 -> 0; matrix products, arithmetic and copies ran while one was open for 0% -> 5% of each run, Pallas kernels for 0% -> 54%
where the time goes in v4:
time: 96.7 us; the launch traced here: 96.5 us
  Pallas kernels  70.2 us (73%)
  between operations  13.4 us (14%)
  local copies, waits for them, and re-layouts  11.1 us (11%)
  other arithmetic  1.77 us (2%)
    pallas_call x1, Pallas kernels, factor(): pl.pallas_call(functools.partial(factor_kernel, strips), out_shape=[jax.S...  29.8 us
    pallas_call x1, Pallas kernels, gather_panel(): pl.pallas_call(functools.partial(gather_kernel, n_wide, n_narrow), out_sh...  22.2 us
    pallas_call x1, Pallas kernels, finish(): pl.pallas_call(functools.partial(finish_kernel, strips, chunks), out_shap...  18.2 us
    broadcast_in_dim x1, local copies, waits for them, and re-layouts, local(): return mine.astype(jnp.float32).transpose(1, 0, 2)[:, :, None, :]  3.48 us
    unnamed x6, local copies, waits for them, and re-layouts  3.35 us
    slice x1, local copies, waits for them, and re-layouts, local(): near = lax.all_gather(own_rows[:half], 'narrow', axis=0, tiled=False)  2.07 us
  transfers between devices with their start and end apart: 1, of which 0 were waited for; matrix products, arithmetic and copies ran while one was open for 5% of the time, Pallas kernels for 54%

profile of v4, /device:TPU:0, one launch (start us, length us, event | category | flops | bytes accessed | tf_op | source)
XLA Modules:
  0.0 96.5 jit_solution(5715714751331920068)
XLA Ops:
  6.5 0.0 all-gather.3.cloned.1.call-start
  6.5 2.1 %fusion.1 = (bf16[256,1,1024]{2,0,1:T(8,128)(2,1)}, bf16[256,1024]{1,0:T(8,128)(2,1)S(1)}) fusion(bf16[512,1,1024]{2,0,1:T(8,128)(2,1)} %param.2), kind=kLoop, calls=%fused_computation.6 | loop fusion | bytes 2097152 | tf_op jit(solution)/shard_map/slice | solution.py:333
  8.6 0.0 all-gather.3.cloned.1.call-update
  8.6 0.8 slice_bitcast_fusion.1.own_ref
  9.5 22.2 %shard_map.28 = bf16[32,32,1024]{2,1,0:T(8,128)(2,1)S(1)} custom-call(bf16[32,1024]{1,0:T(8,128)(2,1)S(1)} %slice_bitcast_fusion.1.own_ref), custom_call_target="tpu_custom_call" | custom-call | tf_op jit(solution)/shard_map/pallas_call | solution.py:82
  31.7 0.2 fusion
  31.9 0.8 copy.9
  32.8 1.1 %reshape.14 = bf16[512,1024]{1,0:T(8,128)(2,1)} reshape(bf16[16,8,4,1024]{3,2,1,0:T(4,128)(2,1)S(1)} %bitcast.17) | data formatting | bytes 2097152 | tf_op jit(solution)/shard_map/reshape | solution.py:336
  33.9 0.0 copy-start.1
  33.9 0.6 copy.7
  34.5 0.6 copy-done.1
  35.1 1.6 %pad_maximum_fusion.panel_ref = bf16[1024,1024]{1,0:T(8,128)(2,1)} fusion(bf16[512,1024]{1,0:T(8,128)(2,1)S(1)} %bitcast.18, bf16[512,1024]{1,0:T(8,128)(2,1)S(1)} %copy-done.1), kind=kLoop, calls=%fused_computation | loop fusion | flops 4194304 | bytes 4194304 | tf_op jit(solution)/shard_map/concatenate | solution.py:338
  36.7 29.8 %shard_map.29 = (f32[512,512]{1,0:T(8,128)S(1)}, f32[512,512]{1,0:T(8,128)S(1)}, f32[512,256]{1,0:T(8,128)S(1)}, bf16[1024,1024]{1,0:T(8,128)(2,1)S(1)}, bf16[1024,1024]{1,0:T(8,128)(2,1)}) custom-call(bf16[1024,1024]{1,0:T(8,128)(2,1)} %pad_maximum_fusion.panel_ref, bf16[1024,1024]{1,0:T(8,128)(2,1)} %metric_ref.1), custom_call_target="tpu_custom_call" | custom-call | tf_op jit(solution)/shard_map/pallas_call | solution.py:214
  66.5 0.0 copy-start
  66.5 1.3 %copy-done = bf16[1024,1024]{1,0:T(8,128)(2,1)} copy-done((bf16[1024,1024]{1,0:T(8,128)(2,1)}, bf16[1024,1024]{1,0:T(8,128)(2,1)S(1)}, u32[]{:S(2)}) %copy-start) | copy-done | bytes 2097176
  67.8 0.0 all-gather.3.cloned.1.call-done
  67.8 18.2 %shard_map.30 = bf16[4,512,256]{2,1,0:T(8,128)(2,1)S(1)} custom-call(bf16[256,1024]{1,0:T(8,128)(2,1)S(1)} %get-tuple-element.18.rows_ref, bf16[4,256,1024]{2,1,0:T(8,128)(2,1)} %bitcast.19, bf16[1024,1024]{1,0:T(8,128)(2,1)} %copy-done, bf16[1024,1024]{1,0:T(8,128)(2,1)} %get-tuple-element.11.low_ref, f32[512,512]{1,0:T(8,128)S(1)} %get-tuple-element.12.solve_ref, ...), custom_call_target="tpu_custom_call" | custom-call | tf_op jit(solution)/shard_map/pallas_call | solution.py:306
  86.0 0.2 convert_bitcast_fusion
  86.2 3.5 %copy.5 = f32[512,4,1,256]{3,2,1,0:T(1,128)} copy(f32[512,4,1,256]{3,0,1,2:T(8,128)S(1)} %convert_bitcast_fusion) | data formatting | bytes 4194304 | tf_op jit(solution)/shard_map/broadcast_in_dim | solution.py:341
Async XLA Ops:
  6.5 61.3 %all-gather.3.cloned.1.call-start = ((), (), s32[]{:S(2)}) async-start(), calls=%async_computation | async-start | bytes 2621440 | tf_op jit(solution)/shard_map/all_gather | solution.py:333
  33.9 1.2 %copy-start.1 = (bf16[512,1024]{1,0:T(8,128)(2,1)S(1)}, bf16[512,1024]{1,0:T(8,128)(2,1)}, u32[]{:S(2)}) copy-start(bf16[512,1024]{1,0:T(8,128)(2,1)} %reshape.14) | copy-start | bytes 3145732
  66.5 1.3 %copy-start = (bf16[1024,1024]{1,0:T(8,128)(2,1)}, bf16[1024,1024]{1,0:T(8,128)(2,1)S(1)}, u32[]{:S(2)}) copy-start(bf16[1024,1024]{1,0:T(8,128)(2,1)S(1)} %get-tuple-element.10.high_ref) | copy-start | bytes 6291460
Sparse Core Ops, SparseCore 0:
  8.9 48.6 all-gather.2
